TPU v7x, 32 devices: a whole 2x2x4 slice. The times are simulated.
32 devices in a mesh: path: 4 (over z), mp: 2 (over core), period: 4 (over y, x).
Axes of the slice: x: 2, y: 2, z: 4, core: 2. Of those that a mesh axis runs over, the one named last changes fastest.
Arguments:
- tiles: bfloat16 [512, 256, 256], P(('path', 'mp')), may hold values from -0.375 to 0.375
- tile_rows: int32 [512], P(('path', 'mp')), may hold values from 0 to 7
- tile_cols: int32 [512], P(('path', 'mp')), may hold values from 0 to 127, as said below
- tile_counts: int32 [8], P(('path', 'mp')), may hold values from 8 to 64, as said below
- data: float32 [32768], P(('period', 'path')), parts along dimension 0, may hold values from -6 to 6
Outputs:
- solution: float32 [262144], P(('period', 'path', 'mp')), parts along dimension 0
- left_vector: float32 [32768], P(('period', 'path')), parts along dimension 0
There are 4 independent parts, one for each index of `period`. A program takes and returns all parts, laid end to end along the dimension named above; an argument that names none is the same for every part. Nothing has to cross between parts.
Inputs may be any that keep to these rules, and one draw needn't show every extreme that they name: `tile_counts`: slots from the strip's count on are unused; some strips are full. `tile_cols`: among all 64 slots of one strip, at most 16 name cell tiles t with the same t // 32, and in every strip some value of t // 32 is named by exactly 16 slots.
All inputs are finite; a program needn't handle non-finite values.
Results may differ from a plain program's by a relative error of at most 0.0066.
Values may be sent and summed in bfloat16 or wider, within the bound.
A program may use at most 64 MiB of HBM per device.

v0:
```python
import jax
import jax.numpy as jnp
from jax import lax
from jax.sharding import PartitionSpec as P

CT_DEV = 32
ITERS = 2


def on_device(tiles, tile_rows, tile_cols, tile_counts, data):
    tile = tiles.shape[1]
    slots = tiles.shape[0]
    row_tiles = data.shape[0] // tile
    npath = lax.axis_size("path")
    limit = max(2, max(slots // 8, (slots + npath - 1) // npath))
    live = lax.iota(jnp.int32, slots) < tile_counts[0]
    row_onehot = (
        (tile_rows[None, :] == lax.iota(jnp.int32, row_tiles)[:, None]) & live[None, :]
    ).astype(jnp.float32)
    owner = tile_cols // CT_DEV
    inside = tile_cols % CT_DEV
    same_owner = (owner[:, None] == owner[None, :]).astype(jnp.int32)
    earlier = (lax.iota(jnp.int32, slots)[None, :] < lax.iota(jnp.int32, slots)[:, None]).astype(
        jnp.int32
    )
    rank = jnp.sum(same_owner * earlier, axis=1)
    target = owner * limit + rank
    place = lax.iota(jnp.int32, npath * limit)[:, None] == target[None, :]
    place_live = (place & live[None, :]).astype(jnp.float32)
    place_all = place.astype(jnp.float32)
    slot_inside = (
        jnp.sum(jnp.where(place, inside[None, :], 0), axis=1)
        - 1
        + jnp.sum(place.astype(jnp.int32), axis=1)
    )
    send_index = jnp.where(jnp.sum(place_live, axis=1) > 0, slot_inside, -1).reshape(npath, limit)

    def forward_prods(picked):
        prods = jnp.einsum("sij,sj->si", tiles, picked, preferred_element_type=jnp.float32)
        local = jnp.dot(row_onehot, prods, precision=lax.Precision.HIGHEST).reshape(-1)
        return lax.psum(local, "mp")

    def backward_prods(left_b):
        picked = left_b.reshape(row_tiles, tile)[tile_rows]
        return jnp.einsum("sij,si->sj", tiles, picked, preferred_element_type=jnp.float32)

    def row_norm(left):
        return jnp.sqrt(lax.psum(jnp.sum(left * left), "path") + 1e-12)

    def col_norm(own):
        return jnp.sqrt(lax.psum(jnp.sum(own * own), ("path", "mp")) + 1e-12)

    def right_step(left, state, beta, asked):
        prods = backward_prods(left.astype(jnp.bfloat16))
        bucket = jnp.dot(place_live, prods, precision=lax.Precision.HIGHEST).reshape(
            npath, limit, tile
        )
        got, asked = (
            lax.all_to_all(bucket, "path", split_axis=0, concat_axis=0, tiled=True),
            lax.all_to_all(send_index, "path", split_axis=0, concat_axis=0, tiled=True),
        )
        pick_own = (asked.reshape(-1)[None, :] == lax.iota(jnp.int32, CT_DEV)[:, None]).astype(
            jnp.float32
        )
        own = jnp.dot(
            pick_own, got.reshape(npath * limit, tile), precision=lax.Precision.HIGHEST
        ).reshape(-1)
        if state is not None:
            own = own - beta * state
        alpha = col_norm(own)
        own = own / alpha
        return (own, own, alpha, asked)

    beta = row_norm(data)
    left = data / beta
    phibar = beta
    asked = send_index
    state, right, alpha, asked = right_step(left, None, beta, asked)
    search = right
    rhobar = alpha
    solution = jnp.zeros_like(right)
    for step in range(ITERS):
        own_b = state.astype(jnp.bfloat16).reshape(CT_DEV, tile)
        pick_out = (asked.reshape(-1)[:, None] == lax.iota(jnp.int32, CT_DEV)[None, :]).astype(
            jnp.bfloat16
        )
        reply = (
            jnp.dot(pick_out, own_b, preferred_element_type=jnp.float32)
            .astype(jnp.bfloat16)
            .reshape(npath, limit, tile)
        )
        back = lax.all_to_all(reply, "path", split_axis=0, concat_axis=0, tiled=True)
        forward_picked = jnp.dot(
            place_all.T.astype(jnp.bfloat16),
            back.reshape(npath * limit, tile),
            preferred_element_type=jnp.float32,
        ).astype(jnp.bfloat16)
        left = forward_prods(forward_picked) - alpha * left
        beta = row_norm(left)
        left = left / beta
        state, right, alpha, asked = right_step(left, state, beta, asked)
        rho = jnp.sqrt(rhobar * rhobar + beta * beta)
        cosine = rhobar / rho
        sine = beta / rho
        theta = sine * alpha
        rhobar = -cosine * alpha
        phi = cosine * phibar
        phibar = sine * phibar
        solution = solution + phi / rho * search
        search = right - theta / rho * search
    total_rows = row_tiles * tile * npath
    return (solution, left * jnp.sqrt(jnp.float32(total_rows)))


def solution(mesh):
    placed = (
        P(("path", "mp"), None, None),
        P(("path", "mp")),
        P(("path", "mp")),
        P(("path", "mp")),
        P(("period", "path")),
    )
    return jax.shard_map(
        on_device,
        mesh=mesh,
        in_specs=placed,
        out_specs=(P(("period", "path", "mp")), P(("period", "path"))),
        check_vma=False,
    )
```

profile of v0, /device:TPU:0, one launch (start us, length us, event | category | flops | bytes accessed | tf_op | source)
XLA Modules:
  0.0 143.9 jit_solution(3259545665614137086)
XLA Ops:
  3.1 1.3 multiply_reduce_fusion.4
  4.4 6.3 %all-to-all-start = ((s32[4,1,16]{2,1,0:T(1,128)}), s32[4,1,16]{2,1,0:T(1,128)S(1)}, u32[]{:S(2)}, u32[]{:S(2)}) async-start(s32[4,1,16]{2,1,0:T(1,128)} %bitcast.1), calls=%async_computation | async-start | bytes 4096 | tf_op jit(solution)/shard_map/all_to_all | solution.py:60
  10.7 12.8 %psum.49 = f32[]{:T(128)} all-reduce(f32[]{:T(128)} %multiply_reduce_fusion.4), channel_id=1, replica_groups=mesh['path'=4,'mp'=2,'period'=4] {'path'}, use_global_device_ids=true, to_apply=%region_5.6 | all-reduce | flops 1 | bytes 8 | tf_op jit(solution)/shard_map/psum | solution.py:48
  24.2 0.7 fusion.39
  26.3 4.6 %fusion.18 = f32[64,1,256]{2,1,0:T(1,128)S(1)} fusion(bf16[64,256,256]{2,1,0:T(8,128)(2,1)} %param.5, bf16[64,256,1]{1,0,2:T(8,128)(2,1)S(1)} %bitcast.47), kind=kOutput, calls=%fused_computation.27 | convolution fusion | flops 8388608 | bytes 8486912 | tf_op jit(solution)/shard_map/sij,si->sj/dot_general | solution.py:45
  30.8 0.8 fusion.6
  31.6 3.3 %all-to-all-start.1 = ((f32[4,16,256]{2,1,0:T(8,128)}), f32[4,16,256]{2,1,0:T(8,128)S(1)}, u32[]{:S(2)}, u32[]{:S(2)}) async-start(f32[4,16,256]{2,1,0:T(8,128)} %bitcast.4), calls=%async_computation.1 | async-start | bytes 131072 | tf_op jit(solution)/shard_map/all_to_all | solution.py:59
  36.2 4.4 %all-to-all-done.1 = f32[4,16,256]{2,1,0:T(8,128)S(1)} async-done(((f32[4,16,256]{2,1,0:T(8,128)}), f32[4,16,256]{2,1,0:T(8,128)S(1)}, u32[]{:S(2)}, u32[]{:S(2)}) %all-to-all-start.1) | async-done | bytes 65568 | tf_op jit(solution)/shard_map/all_to_all | solution.py:59
  40.6 0.7 multiply_reduce_fusion.1
  41.4 14.2 %psum.50 = f32[]{:T(128)} all-reduce(f32[]{:T(128)} %get-tuple-element.8), channel_id=1, replica_groups=mesh['path'=4,'mp'=2,'period'=4] {'path','mp'}, use_global_device_ids=true, to_apply=%region_7.8 | all-reduce | flops 1 | bytes 8 | tf_op jit(solution)/shard_map/psum | solution.py:51
  56.5 8.0 %all_to_all.27 = bf16[4,16,256]{2,1,0:T(8,128)(2,1)S(1)} all-to-all(bf16[4,16,256]{2,1,0:T(8,128)(2,1)S(1)} %bitcast.54), channel_id=1, replica_groups=mesh['path'=4,'mp'=2,'period'=4] {'path'}, dimensions={0} | all-to-all | bytes 65536 | tf_op jit(solution)/shard_map/all_to_all | solution.py:92
  64.7 5.6 %fusion.15 = f32[64,1,256]{2,1,0:T(1,128)S(1)} fusion(bf16[64,256,256]{2,1,0:T(8,128)(2,1)} %param.5, bf16[64,256,1]{1,0,2:T(8,128)(2,1)S(1)} %fusion), kind=kOutput, calls=%fused_computation.24 | convolution fusion | flops 8388608 | bytes 8486912 | tf_op jit(solution)/shard_map/sij,sj->si/dot_general | solution.py:39
  70.5 2.5 %psum.51 = f32[2048]{0:T(1024)S(1)} all-reduce(f32[2048]{0:T(1024)S(1)} %bitcast.55), channel_id=1, replica_groups=mesh['path'=4,'mp'=2,'period'=4] {'mp'}, use_global_device_ids=true, to_apply=%region_8.9 | all-reduce | flops 2048 | bytes 16384 | tf_op jit(solution)/shard_map/psum | solution.py:41
  73.6 9.7 %psum.52 = f32[]{:T(128)} all-reduce(f32[]{:T(128)} %get-tuple-element.4), channel_id=1, replica_groups=mesh['path'=4,'mp'=2,'period'=4] {'path'}, use_global_device_ids=true, to_apply=%region_10.11 | all-reduce | flops 1 | bytes 8 | tf_op jit(solution)/shard_map/psum | solution.py:48
  84.7 4.6 %fusion.12 = f32[64,1,256]{2,1,0:T(1,128)S(1)} fusion(bf16[64,256,256]{2,1,0:T(8,128)(2,1)} %param.5, bf16[64,256,1]{1,0,2:T(8,128)(2,1)S(1)} %bitcast.46), kind=kOutput, calls=%fused_computation.21 | convolution fusion | flops 8388608 | bytes 8486912 | tf_op jit(solution)/shard_map/sij,si->sj/dot_general | solution.py:45
  89.5 8.1 %all_to_all.28 = f32[4,16,256]{2,1,0:T(8,128)S(1)} all-to-all(f32[4,16,256]{2,1,0:T(8,128)S(1)} %bitcast.49), channel_id=1, replica_groups=mesh['path'=4,'mp'=2,'period'=4] {'path'}, dimensions={0} | all-to-all | bytes 131072 | tf_op jit(solution)/shard_map/all_to_all | solution.py:59
  97.6 0.7 multiply_reduce_fusion
  98.3 14.2 %psum.53 = f32[]{:T(128)} all-reduce(f32[]{:T(128)} %get-tuple-element.10), channel_id=1, replica_groups=mesh['path'=4,'mp'=2,'period'=4] {'path','mp'}, use_global_device_ids=true, to_apply=%region_12.13 | all-reduce | flops 1 | bytes 8 | tf_op jit(solution)/shard_map/psum | solution.py:51
  113.2 0.8 convolution_convert_fusion.1
  114.1 3.3 %all-to-all-start.4 = ((bf16[4,16,256]{2,1,0:T(8,128)(2,1)}), bf16[4,16,256]{2,1,0:T(8,128)(2,1)S(1)}, u32[]{:S(2)}, u32[]{:S(2)}) async-start(bf16[4,16,256]{2,1,0:T(8,128)(2,1)} %bitcast.14), calls=%async_computation.4 | async-start | bytes 65536 | tf_op jit(solution)/shard_map/all_to_all | solution.py:92
  117.6 5.4 %all-to-all-done.4 = bf16[4,16,256]{2,1,0:T(8,128)(2,1)S(1)} async-done(((bf16[4,16,256]{2,1,0:T(8,128)(2,1)}), bf16[4,16,256]{2,1,0:T(8,128)(2,1)S(1)}, u32[]{:S(2)}, u32[]{:S(2)}) %all-to-all-start.4) | async-done | bytes 32800 | tf_op jit(solution)/shard_map/all_to_all | solution.py:92
  123.1 5.6 %fusion.9 = f32[64,1,256]{2,1,0:T(1,128)S(1)} fusion(bf16[64,256,256]{2,1,0:T(8,128)(2,1)} %param.5, bf16[64,256,1]{1,0,2:T(8,128)(2,1)S(1)} %fusion.1), kind=kOutput, calls=%fused_computation.18 | convolution fusion | flops 8388608 | bytes 8486912 | tf_op jit(solution)/shard_map/sij,sj->si/dot_general | solution.py:39
  128.9 2.5 %psum.54 = f32[2048]{0:T(1024)S(1)} all-reduce(f32[2048]{0:T(1024)S(1)} %bitcast.56), channel_id=1, replica_groups=mesh['path'=4,'mp'=2,'period'=4] {'mp'}, use_global_device_ids=true, to_apply=%region_13.14 | all-reduce | flops 2048 | bytes 16384 | tf_op jit(solution)/shard_map/psum | solution.py:41
  132.1 9.7 %psum.55 = f32[]{:T(128)} all-reduce(f32[]{:T(128)} %multiply_reduce_fusion.2), channel_id=1, replica_groups=mesh['path'=4,'mp'=2,'period'=4] {'path'}, use_global_device_ids=true, to_apply=%region_15.16 | all-reduce | flops 1 | bytes 8 | tf_op jit(solution)/shard_map/psum | solution.py:48
  (36 shorter events, 8.7 us)
Async XLA Ops:
  4.4 27.3 %all-to-all-start = ((s32[4,1,16]{2,1,0:T(1,128)}), s32[4,1,16]{2,1,0:T(1,128)S(1)}, u32[]{:S(2)}, u32[]{:S(2)}) async-start(s32[4,1,16]{2,1,0:T(1,128)} %bitcast.1), calls=%async_computation | async-start | bytes 4096 | tf_op jit(solution)/shard_map/all_to_all | solution.py:60
  30.8 39.5 %copy-start.1 = (s32[64]{0:T(128)S(1)}, s32[64]{0:T(128)}, u32[]{:S(2)}) copy-start(s32[64]{0:T(128)} %param.6) | copy-start | bytes 772
  30.8 42.2 %copy-start = (f32[2048]{0:T(1024)S(1)}, f32[2048]{0:T(1024)}, u32[]{:S(2)}) copy-start(f32[2048]{0:T(1024)} %param.9) | copy-start | bytes 24580
  31.6 9.0 %all-to-all-start.1 = ((f32[4,16,256]{2,1,0:T(8,128)}), f32[4,16,256]{2,1,0:T(8,128)S(1)}, u32[]{:S(2)}, u32[]{:S(2)}) async-start(f32[4,16,256]{2,1,0:T(8,128)} %bitcast.4), calls=%async_computation.1 | async-start | bytes 131072 | tf_op jit(solution)/shard_map/all_to_all | solution.py:59
  114.1 8.9 %all-to-all-start.4 = ((bf16[4,16,256]{2,1,0:T(8,128)(2,1)}), bf16[4,16,256]{2,1,0:T(8,128)(2,1)S(1)}, u32[]{:S(2)}, u32[]{:S(2)}) async-start(bf16[4,16,256]{2,1,0:T(8,128)(2,1)} %bitcast.14), calls=%async_computation.4 | async-start | bytes 65536 | tf_op jit(solution)/shard_map/all_to_all | solution.py:92
where the time goes:
time: 145 us; the launch traced here: 144 us
  blocking collectives  81.7 us (56%)
  matrix products  24.6 us (17%)
  starting transfers between devices  12.9 us (9%)
  waiting for transfers between devices  9.85 us (7%)
  other arithmetic  6.28 us (4%)
  between operations  5.23 us (4%)
  local copies, waits for them, and re-layouts  3.34 us (2%)
    psum x3, blocking collectives, row_norm(): return jnp.sqrt(lax.psum(jnp.sum(left * left), 'path') + 1e-12)  32.2 us
    psum x2, blocking collectives, col_norm(): return jnp.sqrt(lax.psum(jnp.sum(own * own), ('path', 'mp')) + 1e-12)  28.4 us
    dot_general x2, matrix products, forward_prods(): jnp.einsum('sij,sj->si', tiles, picked, preferred_element_type=jnp.float32)  11.3 us
    dot_general x2, matrix products, backward_prods(): jnp.einsum('sij,si->sj', tiles, picked, preferred_element_type=jnp.float32)  9.15 us
    all_to_all x1, blocking collectives, right_step(): lax.all_to_all(bucket, 'path', split_axis=0, concat_axis=0, tiled=True)  8.11 us
    all_to_all x1, blocking collectives, on_device(): lax.all_to_all(reply, 'path', split_axis=0, concat_axis=0, tiled=True)  8.01 us
    all_to_all x1, starting transfers between devices, right_step(): lax.all_to_all(send_index, 'path', split_axis=0, concat_axis=0, tiled=True)  6.32 us
    all_to_all x1, waiting for transfers between devices, on_device(): lax.all_to_all(reply, 'path', split_axis=0, concat_axis=0, tiled=True)  5.4 us
  transfers between devices with their start and end apart: 3, of which 2 were waited for; matrix products, arithmetic and copies ran while one was open for 6% of the time, Pallas kernels for 0%

commit v1 on v0

v1 whole, which is shorter than its diff:
```python
import functools

import jax
import jax.numpy as jnp
from jax import lax
from jax.experimental import pallas as pl
from jax.experimental.pallas import tpu as pltpu
from jax.sharding import PartitionSpec as P

CT_DEV = 32
CHUNK = 16
GROUP = 8
F32 = jnp.float32
BF16 = jnp.bfloat16


def iota(shape, dim):
    return lax.broadcasted_iota(jnp.int32, shape, dim)


def total(x):
    return jnp.sum(jnp.sum(x, axis=0, keepdims=True), axis=1, keepdims=True)


def split(x):
    hi = x.astype(BF16).astype(F32)
    return hi, x - hi


def kernel(
    npath,
    tiles_hbm,
    rows_ref,
    cols_ref,
    counts_ref,
    data_ref,
    sol_ref,
    left_ref,
    state_ref,
    scal_ref,
    tiles,
    info,
    terms,
    halves_out,
    halves_in,
    sums,
    picks,
    spread,
    lhs,
    prior,
    tile_sem,
    info_sem,
    term_sem,
    half_sem,
    sum_sem,
):
    slots, tile = tiles.shape[0], tiles.shape[1]
    groups, chunks = slots // GROUP, slots // CHUNK
    width = npath * slots
    cells = npath * CT_DEV
    expanded = slots * GROUP
    me = lax.axis_index("path")
    mp = lax.axis_index("mp")

    def tile_copy(g):
        part = pl.ds(g * GROUP, GROUP)
        return pltpu.make_async_copy(tiles_hbm.at[part], tiles.at[part], tile_sem.at[g])

    def peer(step):
        return lax.rem(me + step, npath)

    def sender(step):
        return lax.rem(me + npath - step, npath)

    def to_peer(src, dst, sems, index, step):
        return pltpu.make_async_remote_copy(
            src_ref=src,
            dst_ref=dst,
            send_sem=sems.at[(0, *index)],
            recv_sem=sems.at[(1, *index)],
            device_id={"path": peer(step)},
            device_id_type=pl.DeviceIdType.MESH,
        )

    for g in range(groups):
        tile_copy(g).start()

    barrier = pltpu.get_barrier_semaphore()
    for step in range(1, npath):
        pl.semaphore_signal(
            barrier, inc=1, device_id={"path": peer(step)}, device_id_type=pl.DeviceIdType.MESH
        )
    pl.semaphore_signal(
        barrier, inc=1, device_id={"mp": 1 - mp}, device_id_type=pl.DeviceIdType.MESH
    )

    half_rows = data_ref.shape[0] // 2
    data = jnp.concatenate(
        [data_ref[pl.ds(0, half_rows, stride=2), :], data_ref[pl.ds(1, half_rows, stride=2), :]],
        axis=1,
    )
    live = iota((1, slots), 1) < counts_ref[0]
    row_code = jnp.where(live, rows_ref[...], -1).astype(F32)
    col_live = jnp.where(live, cols_ref[...], -1).astype(F32)

    diag = iota((slots, slots), 0) == iota((slots, slots), 1)
    col_down = jnp.sum(jnp.where(diag, col_live, 0.0), axis=1, keepdims=True)
    here = iota((slots, width), 1) - me * slots == iota((slots, width), 0)
    placed = jnp.sum(jnp.where(here, col_down, 0.0), axis=0, keepdims=True)
    line = iota((8, width), 0)
    info[me] = jnp.where(line == 0, placed, jnp.where(line == 1, total(data * data), 0.0))

    pl.semaphore_wait(barrier, npath)

    def info_copy(step):
        return to_peer(info.at[me], info.at[me], info_sem, (step,), step)

    for step in range(1, npath):
        info_copy(step).start()

    q = iota((2 * slots, slots), 0)
    slot_of_q = q // 16 * 8 + q % 8
    row_q = jnp.sum(
        jnp.where(slot_of_q == iota((2 * slots, slots), 1), row_code, 0.0), axis=1, keepdims=True
    )
    qc = iota((2 * slots, 16), 0)
    offset = (qc % 16 // 8 * 8).astype(F32)
    pick_rows = ((row_q + offset == iota((2 * slots, 16), 1).astype(F32)) & (row_q >= 0)).astype(BF16)

    def term_copy(which, chunk, step):
        part = pl.ds(chunk * CHUNK, CHUNK)
        ref = terms.at[which, me, part]
        return to_peer(ref, ref, term_sem, (which, chunk, step), step)

    def norm_copy(step):
        ref = terms.at[1, me, pl.ds(slots, 16)]
        return to_peer(ref, ref, term_sem, (1, chunks, step), step)

    def backward(which, left):
        hi, lo = split(left)
        both = jnp.concatenate([hi, lo], axis=0).astype(BF16)
        picks[...] = jnp.dot(pick_rows, both, preferred_element_type=F32).astype(BF16)

        def one_chunk(chunk, carry):
            parts = []
            for half in range(CHUNK // GROUP):
                g = chunk * (CHUNK // GROUP) + half
                if which == 0:
                    tile_copy(g).wait()
                block = picks[pl.ds(pl.multiple_of(g * 16, 16), 16), :].astype(F32)
                spot = iota((16, tile), 0) % 8
                acc = jnp.zeros((16, tile), F32)
                for k in range(GROUP):
                    row = jnp.where(spot == k, block, 0.0).astype(BF16)
                    acc = acc + jnp.dot(row, tiles[g * GROUP + k], preferred_element_type=F32)
                parts.append(acc[:8] + acc[8:])
            start = pl.multiple_of(chunk * CHUNK, CHUNK)
            terms[which, me, pl.ds(start, CHUNK), :] = jnp.concatenate(parts, axis=0).astype(BF16)
            for step in range(1, npath):
                term_copy(which, chunk, step).start()
            return carry

        lax.fori_loop(0, chunks, one_chunk, 0)

    def wait_terms(which):
        for chunk in range(chunks):
            for step in range(1, npath):
                term_copy(which, chunk, step).wait()

    def gathered(which):
        block = terms[which, :, :slots, :].reshape(width, tile)
        return jnp.dot(spread[...], block, preferred_element_type=F32)

    def forward(which, right):
        hi, lo = split(right[:expanded].reshape(slots, GROUP, tile))
        lhs[...] = jnp.concatenate([hi, lo], axis=1).astype(BF16)

        def one_group(g, acc):
            for k in range(GROUP):
                s = g * GROUP + k
                acc = acc + lax.dot_general(
                    lhs[s], tiles[s], (((1,), (1,)), ((), ())), preferred_element_type=F32
                )
            return acc

        acc = lax.fori_loop(0, groups, one_group, jnp.zeros((16, tile), F32))
        rest = right[expanded:]
        mine = acc[:8] + acc[8:]
        norm = jnp.broadcast_to(total(rest * rest), (8, 128))
        halves_out[which] = jnp.concatenate([mine, norm], axis=1)
        copy = pltpu.make_async_remote_copy(
            src_ref=halves_out.at[which],
            dst_ref=halves_in.at[which],
            send_sem=half_sem.at[0, which],
            recv_sem=half_sem.at[1, which],
            device_id={"mp": 1 - mp},
            device_id_type=pl.DeviceIdType.MESH,
        )
        copy.start()
        copy.wait()
        both = halves_out[which] + halves_in[which]
        return both[:, :tile], jnp.sqrt(both[:1, tile : tile + 1] + 1e-12)

    backward(0, data)

    for step in range(1, npath):
        info_copy(step).wait()
    facts = info[0]
    for p in range(1, npath):
        facts = facts + info[p]
    all_cols = facts[:1]
    beta0 = jnp.sqrt(facts[1:2, :1] + 1e-12)

    e = iota((expanded, slots), 0)
    mine = iota((expanded, slots), 1) == e // GROUP
    wanted = jnp.where(
        row_code == (e % GROUP).astype(F32), jnp.maximum(cols_ref[...].astype(F32), 0.0), -2.0
    )
    wanted = jnp.sum(jnp.where(mine, wanted, 0.0), axis=1, keepdims=True)
    spread[:expanded] = (wanted == all_cols).astype(BF16)
    spread[expanded:] = (iota((cells, width), 0).astype(F32) == all_cols).astype(BF16)

    wait_terms(0)
    right = gathered(0) / beta0
    prior[...] = right
    product, alpha0 = forward(0, right)
    left0 = data / beta0
    left = product / alpha0 - alpha0 * left0
    n0, n1 = split(total(left * left))
    n1, n2 = split(n1)
    line = iota((16, tile), 0)
    terms[1, me, slots:, :] = jnp.where(
        line == 0, n0, jnp.where(line == 1, n1, jnp.where(line == 2, n2, 0.0))
    ).astype(BF16)
    for step in range(1, npath):
        norm_copy(step).start()
    backward(1, left)
    for step in range(1, npath):
        norm_copy(step).wait()
    norms = jnp.sum(terms[1, :, slots:, :128].astype(F32).reshape(npath * 16, 128), axis=0, keepdims=True)
    beta1 = jnp.sqrt(norms[:, :1] + 1e-12)
    left = left / beta1
    wait_terms(1)
    right = gathered(1) / beta1 - (beta1 / alpha0) * prior[...]
    own = pl.ds(expanded + me * CT_DEV, CT_DEV)
    search = prior[own, :] / alpha0
    prior[...] = right
    product, alpha1 = forward(1, right)
    left = product / alpha1 - alpha1 * left
    sums[me] = jnp.broadcast_to(total(left * left), (8, 128))

    def sum_copy(step):
        return to_peer(sums.at[me], sums.at[me], sum_sem, (step,), step)

    for step in range(1, npath):
        sum_copy(step).start()

    state = prior[own, :] / alpha1
    rho = jnp.sqrt(alpha0 * alpha0 + beta1 * beta1)
    cosine, sine = alpha0 / rho, beta1 / rho
    theta = sine * alpha1
    rhobar = -cosine * alpha1
    phi = cosine * beta0
    phibar = sine * beta0
    first = phi / rho * search
    search = state - theta / rho * search
    state_ref[...] = state

    for step in range(1, npath):
        sum_copy(step).wait()
    norm = sums[0]
    for p in range(1, npath):
        norm = norm + sums[p]
    beta2 = jnp.sqrt(norm[:1, :1] + 1e-12)
    left = left / beta2 * jnp.sqrt(F32(npath * half_rows * tile))
    rho = jnp.sqrt(rhobar * rhobar + beta2 * beta2)
    phi = rhobar / rho * phibar
    answer = first + phi / rho * search
    for h in range(2):
        cut = slice(h * 128, h * 128 + 128)
        sol_ref[pl.ds(h, CT_DEV, stride=2), :] = answer[:, cut]
        left_ref[pl.ds(h, half_rows, stride=2), :] = left[:, cut]
    scal_ref[...] = jnp.broadcast_to(beta2, scal_ref.shape)


def last_right_step(tiles, tile_rows, tile_cols, tile_counts, left, beta, state):
    slots, tile = tiles.shape[0], tiles.shape[1]
    npath = lax.axis_size("path")
    live = lax.iota(jnp.int32, slots) < tile_counts[0]
    picked = left.reshape(-1, tile).astype(BF16)[tile_rows]
    prods = jnp.einsum("sij,si->sj", tiles, picked, preferred_element_type=F32)
    place = (lax.iota(jnp.int32, npath * CT_DEV)[:, None] == tile_cols[None, :]) & live[None, :]
    cells = jnp.dot(place.astype(F32), prods, precision=lax.Precision.HIGHEST)
    own = lax.psum_scatter(cells, "path", scatter_dimension=0, tiled=True) - beta * state
    alpha = jnp.sqrt(lax.psum(jnp.sum(own * own), ("path", "mp")) + 1e-12)
    return own / alpha, alpha


def on_device(tiles, tile_rows, tile_cols, tile_counts, data):
    slots, tile = tiles.shape[0], tiles.shape[1]
    npath = lax.axis_size("path")
    row_tiles = data.shape[0] // tile
    width, lines = npath * slots, slots * GROUP + npath * CT_DEV
    chunks = slots // CHUNK
    vmem = pl.BlockSpec(memory_space=pltpu.VMEM)
    answer, left, state, beta = pl.pallas_call(
        functools.partial(kernel, npath),
        out_shape=(
            jax.ShapeDtypeStruct((CT_DEV * tile // 128, 128), F32),
            jax.ShapeDtypeStruct((row_tiles * tile // 128, 128), F32),
            jax.ShapeDtypeStruct((CT_DEV, tile), F32),
            jax.ShapeDtypeStruct((8, 128), F32),
        ),
        in_specs=[
            pl.BlockSpec(memory_space=pl.ANY),
            vmem,
            vmem,
            pl.BlockSpec(memory_space=pltpu.SMEM),
            vmem,
        ],
        out_specs=(vmem,) * 4,
        scratch_shapes=[
            pltpu.VMEM((slots, tile, tile), BF16),
            pltpu.VMEM((npath, 8, width), F32),
            pltpu.VMEM((2, npath, slots + 16, tile), BF16),
            pltpu.VMEM((2, 8, tile + 128), F32),
            pltpu.VMEM((2, 8, tile + 128), F32),
            pltpu.VMEM((npath, 8, 128), F32),
            pltpu.VMEM((2 * slots, tile), BF16),
            pltpu.VMEM((lines, width), BF16),
            pltpu.VMEM((slots, 16, tile), BF16),
            pltpu.VMEM((lines, tile), F32),
            pltpu.SemaphoreType.DMA((slots // GROUP,)),
            pltpu.SemaphoreType.DMA((2, npath)),
            pltpu.SemaphoreType.DMA((2, 2, chunks + 1, npath)),
            pltpu.SemaphoreType.DMA((2, 2)),
            pltpu.SemaphoreType.DMA((2, npath)),
        ],
        compiler_params=pltpu.CompilerParams(
            collective_id=0, has_side_effects=True, vmem_limit_bytes=48 * 1024 * 1024
        ),
        cost_estimate=pl.CostEstimate(
            flops=8 * 16 * slots * tile * tile,
            bytes_accessed=2 * slots * tile * tile,
            transcendentals=0,
        ),
    )(
        tiles,
        tile_rows.reshape(1, slots),
        tile_cols.reshape(1, slots),
        tile_counts,
        data.reshape(-1, 128),
    )
    left = left.reshape(-1)
    last_right_step(
        tiles,
        tile_rows,
        tile_cols,
        tile_counts,
        left / jnp.sqrt(F32(row_tiles * tile * npath)),
        beta[0, 0],
        state,
    )
    return answer.reshape(-1), left


def solution(mesh):
    placed = (
        P(("path", "mp"), None, None),
        P(("path", "mp")),
        P(("path", "mp")),
        P(("path", "mp")),
        P(("period", "path")),
    )
    return jax.shard_map(
        on_device,
        mesh=mesh,
        in_specs=placed,
        out_specs=(P(("period", "path", "mp")), P(("period", "path"))),
        check_vma=False,
    )
```

time: 145 us -> 36.2 us (0.25)
  blocking collectives: 81.7 us -> 0 us
  Pallas kernels: 0 us -> 31.4 us
  matrix products: 24.6 us -> 0 us
  starting transfers between devices: 12.9 us -> 0 us
  waiting for transfers between devices: 9.85 us -> 0 us
  other arithmetic: 6.28 us -> 0 us
  between operations: 5.23 us -> 1.3 us
    psum x7 -> x0, blocking collectives: 65.6 us -> none  [the longest x3 32.2 us: row_norm(): return jnp.sqrt(lax.psum(jnp.sum(left * left), 'path') + 1e-12)]
    pallas_call x0 -> x1, Pallas kernels: none -> 31.4 us  [on_device(): pl.pallas_call(functools.partial(kernel, npath), out_shape=(jax.ShapeDtyp...]
    dot_general x14 -> x0, matrix products: 24.6 us -> none  [the longest x2 11.3 us: forward_prods(): jnp.einsum('sij,sj->si', tiles, picked, preferred_element_type=jnp.float32)]
    all_to_all x2 -> x0, blocking collectives: 16.1 us -> none  [the longest x1 8.11 us: right_step(): lax.all_to_all(bucket, 'path', split_axis=0, concat_axis=0, tiled=True)]
    all_to_all x3 -> x0, starting transfers between devices: 12.9 us -> none  [the longest x1 6.32 us: right_step(): lax.all_to_all(send_index, 'path', split_axis=0, concat_axis=0, tiled=True)]
    all_to_all x3 -> x0, waiting for transfers between devices: 9.85 us -> none  [the longest x1 5.4 us: on_device(): lax.all_to_all(reply, 'path', split_axis=0, concat_axis=0, tiled=True)]
    reduce_sum x6 -> x0, other arithmetic: 2.92 us -> none  [the longest x3 2.52 us: row_norm(): return jnp.sqrt(lax.psum(jnp.sum(left * left), 'path') + 1e-12)]
    unnamed x7 -> x8, local copies, waits for them, and re-layouts: 0.66 us -> 3.22 us
  transfers between devices with their start and end apart: 3 -> 0, of which waited for: 2 -> 0; matrix products, arithmetic and copies ran while one was open for 6% -> 0% of each run, Pallas kernels for 0% -> 0%
where the time goes in v1:
time: 36.2 us; the launch traced here: 35.9 us
  Pallas kernels  31.4 us (87%)
  local copies, waits for them, and re-layouts  3.22 us (9%)
  between operations  1.3 us (4%)
    pallas_call x1, Pallas kernels, on_device(): pl.pallas_call(functools.partial(kernel, npath), out_shape=(jax.ShapeDtyp...  31.4 us
    unnamed x8, local copies, waits for them, and re-layouts  3.22 us

profile of v1, /device:TPU:0, one launch (start us, length us, event | category | flops | bytes accessed | tf_op | source)
XLA Modules:
  0.0 35.9 jit_solution(13023495002547710575)
XLA Ops:
  1.3 0.0 copy-start
  1.3 0.7 %copy-done = f32[2048]{0:T(1024)S(1)} copy-done((f32[2048]{0:T(1024)S(1)}, f32[2048]{0:T(1024)}, u32[]{:S(2)}) %copy-start) | copy-done | bytes 8216
  2.0 0.0 copy-start.1
  2.0 0.7 %copy-done.1 = s32[64]{0:T(128)S(1)} copy-done((s32[64]{0:T(128)S(1)}, s32[64]{0:T(128)}, u32[]{:S(2)}) %copy-start.1) | copy-done | bytes 280
  2.6 0.0 copy-start.2
  2.6 0.7 %copy-done.2 = s32[64]{0:T(128)S(1)} copy-done((s32[64]{0:T(128)S(1)}, s32[64]{0:T(128)}, u32[]{:S(2)}) %copy-start.2) | copy-done | bytes 280
  3.3 31.4 %shard_map.68 = (f32[64,128]{1,0:T(8,128)S(1)}, f32[16,128]{1,0:T(8,128)S(1)}, f32[32,256]{1,0:T(8,128)}, f32[8,128]{1,0:T(8,128)}) custom-call(bf16[64,256,256]{2,1,0:T(8,128)(2,1)} %tiles_hbm.1, s32[1,64]{1,0:T(1,128)S(1)} %bitcast.8, s32[1,64]{1,0:T(1,128)S(1)} %bitcast.9, s32[1]{0:T(128)S(6)} %copy.9.counts_ref, f32[16,128]{1,0:T(8,128)S(1)} %bitcast.7), custom_call_target="tpu_custom_call" | custom-call | flops 536870912 | bytes 8388608 | tf_op jit(solution)/shard_map/pallas_call | solution.py:306
  34.7 0.6 %copy.10 = f32[8192]{0:T(1024)} copy(f32[8192]{0:T(1024)S(1)} %bitcast.5) | data formatting | bytes 65536
  35.3 0.6 %copy.11 = f32[2048]{0:T(1024)} copy(f32[2048]{0:T(1024)S(1)} %bitcast.6) | data formatting | bytes 16384
Async XLA Ops:
  1.3 0.7 %copy-start = (f32[2048]{0:T(1024)S(1)}, f32[2048]{0:T(1024)}, u32[]{:S(2)}) copy-start(f32[2048]{0:T(1024)} %param.9) | copy-start | bytes 24580
  2.0 0.7 %copy-start.1 = (s32[64]{0:T(128)S(1)}, s32[64]{0:T(128)}, u32[]{:S(2)}) copy-start(s32[64]{0:T(128)} %param.6) | copy-start | bytes 772
  2.6 0.7 %copy-start.2 = (s32[64]{0:T(128)S(1)}, s32[64]{0:T(128)}, u32[]{:S(2)}) copy-start(s32[64]{0:T(128)} %param.7) | copy-start | bytes 772

commit v2 on v1

--- a/solution.py
+++ b/solution.py
@@ -30,14 +30,16 @@
 def kernel(
     npath,
     tiles_hbm,
+    rows_hbm,
+    cols_hbm,
+    counts_hbm,
+    data_hbm,
+    pack_hbm,
     rows_ref,
     cols_ref,
     counts_ref,
     data_ref,
-    sol_ref,
-    left_ref,
-    state_ref,
-    scal_ref,
+    pack_ref,
     tiles,
     info,
     terms,
@@ -48,6 +50,8 @@
     spread,
     lhs,
     prior,
+    small_sem,
+    out_sem,
     tile_sem,
     info_sem,
     term_sem,
@@ -82,6 +86,19 @@
             device_id_type=pl.DeviceIdType.MESH,
         )
 
+    smalls = [
+        pltpu.make_async_copy(src, dst, small_sem.at[i])
+        for i, (src, dst) in enumerate(
+            (
+                (data_hbm, data_ref),
+                (rows_hbm, rows_ref),
+                (cols_hbm, cols_ref),
+                (counts_hbm, counts_ref),
+            )
+        )
+    ]
+    for copy in smalls:
+        copy.start()
     for g in range(groups):
         tile_copy(g).start()
 
@@ -94,6 +111,8 @@
         barrier, inc=1, device_id={"mp": 1 - mp}, device_id_type=pl.DeviceIdType.MESH
     )
 
+    for copy in smalls:
+        copy.wait()
     half_rows = data_ref.shape[0] // 2
     data = jnp.concatenate(
         [data_ref[pl.ds(0, half_rows, stride=2), :], data_ref[pl.ds(1, half_rows, stride=2), :]],
@@ -264,7 +283,20 @@
     phibar = sine * beta0
     first = phi / rho * search
     search = state - theta / rho * search
-    state_ref[...] = state
+
+    def keep(block, base):
+        lines = block.shape[0]
+        for h in range(2):
+            pack_ref[pl.ds(base + h, lines, stride=2), :] = block[:, h * 128 : h * 128 + 128]
+
+    def pack_copy(base, lines, i):
+        part = pl.ds(base, lines)
+        return pltpu.make_async_copy(pack_ref.at[part], pack_hbm.at[part], out_sem.at[i])
+
+    result_lines = pack_ref.shape[0] - 2 * CT_DEV
+    keep(state, result_lines)
+    state_copy = pack_copy(result_lines, 2 * CT_DEV, 0)
+    state_copy.start()
 
     for step in range(1, npath):
         sum_copy(step).wait()
@@ -276,11 +308,26 @@
     rho = jnp.sqrt(rhobar * rhobar + beta2 * beta2)
     phi = rhobar / rho * phibar
     answer = first + phi / rho * search
-    for h in range(2):
-        cut = slice(h * 128, h * 128 + 128)
-        sol_ref[pl.ds(h, CT_DEV, stride=2), :] = answer[:, cut]
-        left_ref[pl.ds(h, half_rows, stride=2), :] = left[:, cut]
-    scal_ref[...] = jnp.broadcast_to(beta2, scal_ref.shape)
+    keep(answer, 0)
+    keep(left, 2 * CT_DEV)
+    pack_ref[result_lines - 8 : result_lines] = jnp.broadcast_to(beta2, (8, 128))
+    result_copy = pack_copy(0, result_lines, 1)
+    result_copy.start()
+    state_copy.wait()
+    result_copy.wait()
+
+
+def unpack(pack_hbm, answer_hbm, left_hbm, sem):
+    base = 0
+    copies = []
+    for i, ref in enumerate((answer_hbm, left_hbm)):
+        part = pack_hbm.at[pl.ds(base, ref.shape[0])]
+        copies.append(pltpu.make_async_copy(part, ref, sem.at[i]))
+        base += ref.shape[0]
+    for copy in copies:
+        copy.start()
+    for copy in copies:
+        copy.wait()
 
 
 def last_right_step(tiles, tile_rows, tile_cols, tile_counts, left, beta, state):
@@ -302,24 +349,19 @@
     row_tiles = data.shape[0] // tile
     width, lines = npath * slots, slots * GROUP + npath * CT_DEV
     chunks = slots // CHUNK
-    vmem = pl.BlockSpec(memory_space=pltpu.VMEM)
-    answer, left, state, beta = pl.pallas_call(
+    hbm = pl.BlockSpec(memory_space=pltpu.HBM)
+    answer_lines, left_lines = CT_DEV * tile // 128, row_tiles * tile // 128
+    pack = pl.pallas_call(
         functools.partial(kernel, npath),
-        out_shape=(
-            jax.ShapeDtypeStruct((CT_DEV * tile // 128, 128), F32),
-            jax.ShapeDtypeStruct((row_tiles * tile // 128, 128), F32),
-            jax.ShapeDtypeStruct((CT_DEV, tile), F32),
-            jax.ShapeDtypeStruct((8, 128), F32),
-        ),
-        in_specs=[
-            pl.BlockSpec(memory_space=pl.ANY),
-            vmem,
-            vmem,
-            pl.BlockSpec(memory_space=pltpu.SMEM),
-            vmem,
-        ],
-        out_specs=(vmem,) * 4,
+        out_shape=jax.ShapeDtypeStruct((2 * answer_lines + left_lines + 8, 128), F32),
+        in_specs=[hbm] * 5,
+        out_specs=hbm,
         scratch_shapes=[
+            pltpu.VMEM((1, slots), jnp.int32),
+            pltpu.VMEM((1, slots), jnp.int32),
+            pltpu.SMEM((1,), jnp.int32),
+            pltpu.VMEM((left_lines, 128), F32),
+            pltpu.VMEM((2 * answer_lines + left_lines + 8, 128), F32),
             pltpu.VMEM((slots, tile, tile), BF16),
             pltpu.VMEM((npath, 8, width), F32),
             pltpu.VMEM((2, npath, slots + 16, tile), BF16),
@@ -330,6 +372,8 @@
             pltpu.VMEM((lines, width), BF16),
             pltpu.VMEM((slots, 16, tile), BF16),
             pltpu.VMEM((lines, tile), F32),
+            pltpu.SemaphoreType.DMA((4,)),
+            pltpu.SemaphoreType.DMA((2,)),
             pltpu.SemaphoreType.DMA((slots // GROUP,)),
             pltpu.SemaphoreType.DMA((2, npath)),
             pltpu.SemaphoreType.DMA((2, 2, chunks + 1, npath)),
@@ -337,7 +381,7 @@
             pltpu.SemaphoreType.DMA((2, npath)),
         ],
         compiler_params=pltpu.CompilerParams(
-            collective_id=0, has_side_effects=True, vmem_limit_bytes=48 * 1024 * 1024
+            collective_id=0, has_side_effects=True, vmem_limit_bytes=64 * 1024 * 1024 - 65536
         ),
         cost_estimate=pl.CostEstimate(
             flops=8 * 16 * slots * tile * tile,
@@ -351,14 +395,25 @@
         tile_counts,
         data.reshape(-1, 128),
     )
+    answer, left = pl.pallas_call(
+        unpack,
+        out_shape=(
+            jax.ShapeDtypeStruct((answer_lines, 128), F32),
+            jax.ShapeDtypeStruct((left_lines, 128), F32),
+        ),
+        in_specs=[hbm],
+        out_specs=(hbm, hbm),
+        scratch_shapes=[pltpu.SemaphoreType.DMA((2,))],
+    )(pack)
     left = left.reshape(-1)
+    state = pack[answer_lines + left_lines + 8 :].reshape(CT_DEV, tile)
     last_right_step(
         tiles,
         tile_rows,
         tile_cols,
         tile_counts,
         left / jnp.sqrt(F32(row_tiles * tile * npath)),
-        beta[0, 0],
+        pack[answer_lines + left_lines, 0],
         state,
     )
     return answer.reshape(-1), left

time: 36.2 us -> 36.7 us (1.014)
  Pallas kernels: 31.4 us -> 35.2 us
  local copies, waits for them, and re-layouts: 3.22 us -> 0 us
    pallas_call x1 -> x2, Pallas kernels: 31.4 us -> 35.2 us  [the longest x1 32.8 us: on_device(): pl.pallas_call(functools.partial(kernel, npath), out_shape=jax.ShapeDtype...]
    unnamed x8 -> x0, local copies, waits for them, and re-layouts: 3.22 us -> none
where the time goes in v2:
time: 36.7 us; the launch traced here: 36.5 us
  Pallas kernels  35.2 us (96%)
  between operations  1.28 us (3%)
    pallas_call x1, Pallas kernels, on_device(): pl.pallas_call(functools.partial(kernel, npath), out_shape=jax.ShapeDtype...  32.8 us
    pallas_call x1, Pallas kernels, on_device(): pl.pallas_call(unpack, out_shape=(jax.ShapeDtypeStruct((answer_lines, 128...  2.36 us

profile of v2, /device:TPU:0, one launch (start us, length us, event | category | flops | bytes accessed | tf_op | source)
XLA Modules:
  0.0 36.5 jit_solution(7661127581751512042)
XLA Ops:
  1.3 32.8 %shard_map.68.pack_hbm = f32[152,128]{1,0:T(8,128)} custom-call(bf16[64,256,256]{2,1,0:T(8,128)(2,1)} %tiles_hbm.1, s32[1,64]{1,0:T(1,128)} %bitcast.6, s32[1,64]{1,0:T(1,128)} %bitcast.7, s32[1]{0:T(128)S(6)} %copy.7.counts_hbm, f32[16,128]{1,0:T(8,128)} %bitcast.5), custom_call_target="tpu_custom_call" | custom-call | flops 536870912 | bytes 8388608 | tf_op jit(solution)/shard_map/pallas_call | solution.py:354
  34.1 2.4 %shard_map.69 = (f32[64,128]{1,0:T(8,128)}, f32[16,128]{1,0:T(8,128)}) custom-call(f32[152,128]{1,0:T(8,128)} %shard_map.68.pack_hbm), custom_call_target="tpu_custom_call" | custom-call | tf_op jit(solution)/shard_map/pallas_call | solution.py:398

commit v3 on v2

--- a/solution.py
+++ b/solution.py
@@ -10,6 +10,7 @@
 CT_DEV = 32
 CHUNK = 16
 GROUP = 8
+VMEM_LIMIT = 56 * 1024 * 1024
 F32 = jnp.float32
 BF16 = jnp.bfloat16
 
@@ -34,12 +35,11 @@
     cols_hbm,
     counts_hbm,
     data_hbm,
-    pack_hbm,
+    pack_ref,
     rows_ref,
     cols_ref,
     counts_ref,
     data_ref,
-    pack_ref,
     tiles,
     info,
     terms,
@@ -48,10 +48,9 @@
     sums,
     picks,
     spread,
-    lhs,
+    prods,
     prior,
     small_sem,
-    out_sem,
     tile_sem,
     info_sem,
     term_sem,
@@ -62,7 +61,6 @@
     groups, chunks = slots // GROUP, slots // CHUNK
     width = npath * slots
     cells = npath * CT_DEV
-    expanded = slots * GROUP
     me = lax.axis_index("path")
     mp = lax.axis_index("mp")
 
@@ -146,6 +144,17 @@
     offset = (qc % 16 // 8 * 8).astype(F32)
     pick_rows = ((row_q + offset == iota((2 * slots, 16), 1).astype(F32)) & (row_q >= 0)).astype(BF16)
 
+    row_down = jnp.sum(jnp.where(diag, row_code, 0.0), axis=1, keepdims=True)
+    q = iota((slots, 2 * slots), 1)
+    slot_of_q = q // 16 * 8 + q % 8
+    row_q = jnp.sum(
+        jnp.where(slot_of_q == iota((slots, 2 * slots), 0), row_down, 0.0), axis=0, keepdims=True
+    )
+    offset = (iota((16, 2 * slots), 1) % 16 // 8 * 8).astype(F32)
+    sum_rows = (
+        (row_q + offset == iota((16, 2 * slots), 0).astype(F32)) & (row_q >= 0)
+    ).astype(BF16)
+
     def term_copy(which, chunk, step):
         part = pl.ds(chunk * CHUNK, CHUNK)
         ref = terms.at[which, me, part]
@@ -154,6 +163,11 @@
     def norm_copy(step):
         ref = terms.at[1, me, pl.ds(slots, 16)]
         return to_peer(ref, ref, term_sem, (1, chunks, step), step)
+
+    def fan_out(block):
+        spot = iota((16, tile), 0) % 8
+        rows = [jnp.where(spot == k, block, 0.0).astype(BF16) for k in range(GROUP)]
+        return jnp.concatenate(rows, axis=1)
 
     def backward(which, left):
         hi, lo = split(left)
@@ -167,11 +181,11 @@
                 if which == 0:
                     tile_copy(g).wait()
                 block = picks[pl.ds(pl.multiple_of(g * 16, 16), 16), :].astype(F32)
-                spot = iota((16, tile), 0) % 8
-                acc = jnp.zeros((16, tile), F32)
-                for k in range(GROUP):
-                    row = jnp.where(spot == k, block, 0.0).astype(BF16)
-                    acc = acc + jnp.dot(row, tiles[g * GROUP + k], preferred_element_type=F32)
+                acc = jnp.dot(
+                    fan_out(block),
+                    tiles[pl.ds(g * GROUP, GROUP)].reshape(GROUP * tile, tile),
+                    preferred_element_type=F32,
+                )
                 parts.append(acc[:8] + acc[8:])
             start = pl.multiple_of(chunk * CHUNK, CHUNK)
             terms[which, me, pl.ds(start, CHUNK), :] = jnp.concatenate(parts, axis=0).astype(BF16)
@@ -191,19 +205,31 @@
         return jnp.dot(spread[...], block, preferred_element_type=F32)
 
     def forward(which, right):
-        hi, lo = split(right[:expanded].reshape(slots, GROUP, tile))
-        lhs[...] = jnp.concatenate([hi, lo], axis=1).astype(BF16)
-
-        def one_group(g, acc):
-            for k in range(GROUP):
-                s = g * GROUP + k
-                acc = acc + lax.dot_general(
-                    lhs[s], tiles[s], (((1,), (1,)), ((), ())), preferred_element_type=F32
-                )
-            return acc
-
-        acc = lax.fori_loop(0, groups, one_group, jnp.zeros((16, tile), F32))
-        rest = right[expanded:]
+        hi, lo = split(right[:slots].reshape(groups, GROUP, tile))
+        both = jnp.concatenate([hi, lo], axis=1)
+        picks[...] = both.reshape(2 * slots, tile).astype(BF16)
+
+        def two_groups(pair, carry):
+            for half in range(2):
+                g = pair * 2 + half
+                block = picks[pl.ds(pl.multiple_of(g * 16, 16), 16), :].astype(F32)
+                wide = fan_out(block)
+                acc = jnp.zeros((16, tile), F32)
+                for k in range(GROUP):
+                    acc = acc + lax.dot_general(
+                        wide[:, k * tile : k * tile + tile],
+                        tiles[g * GROUP + k],
+                        (((1,), (1,)), ((), ())),
+                        preferred_element_type=F32,
+                    )
+                prods[g] = acc[:8] + acc[8:]
+            return carry
+
+        lax.fori_loop(0, groups // 2, two_groups, 0)
+        hi, lo = split(prods[...])
+        both = jnp.concatenate([hi, lo], axis=1).reshape(2 * slots, tile).astype(BF16)
+        acc = jnp.dot(sum_rows, both, preferred_element_type=F32)
+        rest = right[slots:]
         mine = acc[:8] + acc[8:]
         norm = jnp.broadcast_to(total(rest * rest), (8, 128))
         halves_out[which] = jnp.concatenate([mine, norm], axis=1)
@@ -230,14 +256,11 @@
     all_cols = facts[:1]
     beta0 = jnp.sqrt(facts[1:2, :1] + 1e-12)
 
-    e = iota((expanded, slots), 0)
-    mine = iota((expanded, slots), 1) == e // GROUP
-    wanted = jnp.where(
-        row_code == (e % GROUP).astype(F32), jnp.maximum(cols_ref[...].astype(F32), 0.0), -2.0
-    )
-    wanted = jnp.sum(jnp.where(mine, wanted, 0.0), axis=1, keepdims=True)
-    spread[:expanded] = (wanted == all_cols).astype(BF16)
-    spread[expanded:] = (iota((cells, width), 0).astype(F32) == all_cols).astype(BF16)
+    col_all_down = jnp.sum(
+        jnp.where(diag, cols_ref[...].astype(F32), 0.0), axis=1, keepdims=True
+    )
+    spread[:slots] = (col_all_down == all_cols).astype(BF16)
+    spread[slots:] = (iota((cells, width), 0).astype(F32) == all_cols).astype(BF16)
 
     wait_terms(0)
     right = gathered(0) / beta0
@@ -261,7 +284,7 @@
     left = left / beta1
     wait_terms(1)
     right = gathered(1) / beta1 - (beta1 / alpha0) * prior[...]
-    own = pl.ds(expanded + me * CT_DEV, CT_DEV)
+    own = pl.ds(slots + me * CT_DEV, CT_DEV)
     search = prior[own, :] / alpha0
     prior[...] = right
     product, alpha1 = forward(1, right)
@@ -289,14 +312,8 @@
         for h in range(2):
             pack_ref[pl.ds(base + h, lines, stride=2), :] = block[:, h * 128 : h * 128 + 128]
 
-    def pack_copy(base, lines, i):
-        part = pl.ds(base, lines)
-        return pltpu.make_async_copy(pack_ref.at[part], pack_hbm.at[part], out_sem.at[i])
-
     result_lines = pack_ref.shape[0] - 2 * CT_DEV
     keep(state, result_lines)
-    state_copy = pack_copy(result_lines, 2 * CT_DEV, 0)
-    state_copy.start()
 
     for step in range(1, npath):
         sum_copy(step).wait()
@@ -311,17 +328,13 @@
     keep(answer, 0)
     keep(left, 2 * CT_DEV)
     pack_ref[result_lines - 8 : result_lines] = jnp.broadcast_to(beta2, (8, 128))
-    result_copy = pack_copy(0, result_lines, 1)
-    result_copy.start()
-    state_copy.wait()
-    result_copy.wait()
-
-
-def unpack(pack_hbm, answer_hbm, left_hbm, sem):
+
+
+def unpack(pack_ref, answer_hbm, left_hbm, sem):
     base = 0
     copies = []
     for i, ref in enumerate((answer_hbm, left_hbm)):
-        part = pack_hbm.at[pl.ds(base, ref.shape[0])]
+        part = pack_ref.at[pl.ds(base, ref.shape[0])]
         copies.append(pltpu.make_async_copy(part, ref, sem.at[i]))
         base += ref.shape[0]
     for copy in copies:
@@ -347,21 +360,21 @@
     slots, tile = tiles.shape[0], tiles.shape[1]
     npath = lax.axis_size("path")
     row_tiles = data.shape[0] // tile
-    width, lines = npath * slots, slots * GROUP + npath * CT_DEV
+    width, lines = npath * slots, slots + npath * CT_DEV
     chunks = slots // CHUNK
     hbm = pl.BlockSpec(memory_space=pltpu.HBM)
+    vmem = pl.BlockSpec(memory_space=pltpu.VMEM)
     answer_lines, left_lines = CT_DEV * tile // 128, row_tiles * tile // 128
     pack = pl.pallas_call(
         functools.partial(kernel, npath),
-        out_shape=jax.ShapeDtypeStruct((2 * answer_lines + left_lines + 8, 128), F32),
+        out_shape=pltpu.VMEM((2 * answer_lines + left_lines + 8, 128), F32),
         in_specs=[hbm] * 5,
-        out_specs=hbm,
+        out_specs=vmem,
         scratch_shapes=[
             pltpu.VMEM((1, slots), jnp.int32),
             pltpu.VMEM((1, slots), jnp.int32),
             pltpu.SMEM((1,), jnp.int32),
             pltpu.VMEM((left_lines, 128), F32),
-            pltpu.VMEM((2 * answer_lines + left_lines + 8, 128), F32),
             pltpu.VMEM((slots, tile, tile), BF16),
             pltpu.VMEM((npath, 8, width), F32),
             pltpu.VMEM((2, npath, slots + 16, tile), BF16),
@@ -370,10 +383,9 @@
             pltpu.VMEM((npath, 8, 128), F32),
             pltpu.VMEM((2 * slots, tile), BF16),
             pltpu.VMEM((lines, width), BF16),
-            pltpu.VMEM((slots, 16, tile), BF16),
+            pltpu.VMEM((slots // GROUP, GROUP, tile), F32),
             pltpu.VMEM((lines, tile), F32),
             pltpu.SemaphoreType.DMA((4,)),
-            pltpu.SemaphoreType.DMA((2,)),
             pltpu.SemaphoreType.DMA((slots // GROUP,)),
             pltpu.SemaphoreType.DMA((2, npath)),
             pltpu.SemaphoreType.DMA((2, 2, chunks + 1, npath)),
@@ -381,7 +393,7 @@
             pltpu.SemaphoreType.DMA((2, npath)),
         ],
         compiler_params=pltpu.CompilerParams(
-            collective_id=0, has_side_effects=True, vmem_limit_bytes=64 * 1024 * 1024 - 65536
+            collective_id=0, has_side_effects=True, vmem_limit_bytes=VMEM_LIMIT
         ),
         cost_estimate=pl.CostEstimate(
             flops=8 * 16 * slots * tile * tile,
@@ -401,7 +413,7 @@
             jax.ShapeDtypeStruct((answer_lines, 128), F32),
             jax.ShapeDtypeStruct((left_lines, 128), F32),
         ),
-        in_specs=[hbm],
+        in_specs=[vmem],
         out_specs=(hbm, hbm),
         scratch_shapes=[pltpu.SemaphoreType.DMA((2,))],
     )(pack)

time: 36.7 us -> 34.8 us (0.948)
  Pallas kernels: 35.2 us -> 32.7 us
  local copies, waits for them, and re-layouts: 0 us -> 0.61 us
    pallas_call x1, Pallas kernels: 32.8 us -> 31.2 us  [on_device(): pl.pallas_call(functools.partial(kernel, npath), out_shape=pltpu.VMEM((2...]
    pallas_call x1, Pallas kernels: 2.36 us -> 1.52 us  [on_device(): pl.pallas_call(unpack, out_shape=(jax.ShapeDtypeStruct((answer_lines, 128...]
    unnamed x0 -> x2, local copies, waits for them, and re-layouts: none -> 0.61 us
where the time goes in v3:
time: 34.8 us; the launch traced here: 34.6 us
  Pallas kernels  32.7 us (94%)
  between operations  1.29 us (4%)
  local copies, waits for them, and re-layouts  0.61 us (2%)
    pallas_call x1, Pallas kernels, on_device(): pl.pallas_call(functools.partial(kernel, npath), out_shape=pltpu.VMEM((2...  31.2 us
    pallas_call x1, Pallas kernels, on_device(): pl.pallas_call(unpack, out_shape=(jax.ShapeDtypeStruct((answer_lines, 128...  1.52 us

profile of v3, /device:TPU:0, one launch (start us, length us, event | category | flops | bytes accessed | tf_op | source)
XLA Modules:
  0.0 34.6 jit_solution(7049096229214631463)
XLA Ops:
  1.3 31.2 %shard_map.68.pack_ref = f32[152,128]{1,0:T(8,128)S(1)} custom-call(bf16[64,256,256]{2,1,0:T(8,128)(2,1)} %tiles_hbm.1, s32[1,64]{1,0:T(1,128)} %bitcast.6, s32[1,64]{1,0:T(1,128)} %bitcast.7, s32[1]{0:T(128)S(6)} %copy.7.counts_hbm, f32[16,128]{1,0:T(8,128)} %bitcast.5), custom_call_target="tpu_custom_call" | custom-call | flops 536870912 | bytes 8388608 | tf_op jit(solution)/shard_map/pallas_call | solution.py:368
  32.5 0.0 copy-start
  32.5 0.6 %copy-done = f32[152,128]{1,0:T(8,128)} copy-done((f32[152,128]{1,0:T(8,128)}, f32[152,128]{1,0:T(8,128)S(1)}, u32[]{:S(2)}) %copy-start) | copy-done | bytes 77848
  33.1 1.5 %shard_map.69 = (f32[64,128]{1,0:T(8,128)}, f32[16,128]{1,0:T(8,128)}) custom-call(f32[152,128]{1,0:T(8,128)} %copy-done), custom_call_target="tpu_custom_call" | custom-call | tf_op jit(solution)/shard_map/pallas_call | solution.py:410
Async XLA Ops:
  32.5 0.6 %copy-start = (f32[152,128]{1,0:T(8,128)}, f32[152,128]{1,0:T(8,128)S(1)}, u32[]{:S(2)}) copy-start(f32[152,128]{1,0:T(8,128)S(1)} %shard_map.68.pack_ref) | copy-start | bytes 233476

commit v4 on v3

--- a/solution.py
+++ b/solution.py
@@ -74,13 +74,13 @@
     def sender(step):
         return lax.rem(me + npath - step, npath)
 
-    def to_peer(src, dst, sems, index, step):
+    def to_peer(src, dst, sems, index, step, **other):
         return pltpu.make_async_remote_copy(
             src_ref=src,
             dst_ref=dst,
             send_sem=sems.at[(0, *index)],
             recv_sem=sems.at[(1, *index)],
-            device_id={"path": peer(step)},
+            device_id={"path": peer(step), **other},
             device_id_type=pl.DeviceIdType.MESH,
         )
 
@@ -102,9 +102,13 @@
 
     barrier = pltpu.get_barrier_semaphore()
     for step in range(1, npath):
-        pl.semaphore_signal(
-            barrier, inc=1, device_id={"path": peer(step)}, device_id_type=pl.DeviceIdType.MESH
-        )
+        for side in (mp, 1 - mp):
+            pl.semaphore_signal(
+                barrier,
+                inc=1,
+                device_id={"path": peer(step), "mp": side},
+                device_id_type=pl.DeviceIdType.MESH,
+            )
     pl.semaphore_signal(
         barrier, inc=1, device_id={"mp": 1 - mp}, device_id_type=pl.DeviceIdType.MESH
     )
@@ -127,7 +131,7 @@
     line = iota((8, width), 0)
     info[me] = jnp.where(line == 0, placed, jnp.where(line == 1, total(data * data), 0.0))
 
-    pl.semaphore_wait(barrier, npath)
+    pl.semaphore_wait(barrier, 2 * npath - 1)
 
     def info_copy(step):
         return to_peer(info.at[me], info.at[me], info_sem, (step,), step)
@@ -204,6 +208,11 @@
         block = terms[which, :, :slots, :].reshape(width, tile)
         return jnp.dot(spread[...], block, preferred_element_type=F32)
 
+    def sum_copy(step, far):
+        ref = sums.at[me, mp]
+        side = 1 - mp if far else mp
+        return to_peer(ref, ref, sum_sem, (far, step), step, mp=side)
+
     def forward(which, right):
         hi, lo = split(right[:slots].reshape(groups, GROUP, tile))
         both = jnp.concatenate([hi, lo], axis=1)
@@ -242,6 +251,11 @@
             device_id_type=pl.DeviceIdType.MESH,
         )
         copy.start()
+        if which == 1:
+            sums[me, mp] = jnp.concatenate([mine[:, :128], mine[:, 128:]], axis=0).astype(BF16)
+            for step in range(1, npath):
+                for far in range(2):
+                    sum_copy(step, far).start()
         copy.wait()
         both = halves_out[which] + halves_in[which]
         return both[:, :tile], jnp.sqrt(both[:1, tile : tile + 1] + 1e-12)
@@ -268,19 +282,15 @@
     product, alpha0 = forward(0, right)
     left0 = data / beta0
     left = product / alpha0 - alpha0 * left0
-    n0, n1 = split(total(left * left))
-    n1, n2 = split(n1)
-    line = iota((16, tile), 0)
-    terms[1, me, slots:, :] = jnp.where(
-        line == 0, n0, jnp.where(line == 1, n1, jnp.where(line == 2, n2, 0.0))
-    ).astype(BF16)
+    terms[1, me, slots:, :] = jnp.concatenate(split(left), axis=0).astype(BF16)
     for step in range(1, npath):
         norm_copy(step).start()
     backward(1, left)
     for step in range(1, npath):
         norm_copy(step).wait()
-    norms = jnp.sum(terms[1, :, slots:, :128].astype(F32).reshape(npath * 16, 128), axis=0, keepdims=True)
-    beta1 = jnp.sqrt(norms[:, :1] + 1e-12)
+    lefts = terms[1, :, slots:, :].astype(F32)
+    lefts = lefts[:, :8] + lefts[:, 8:]
+    beta1 = jnp.sqrt(total(jnp.sum(lefts * lefts, axis=0)) + 1e-12)
     left = left / beta1
     wait_terms(1)
     right = gathered(1) / beta1 - (beta1 / alpha0) * prior[...]
@@ -289,14 +299,6 @@
     prior[...] = right
     product, alpha1 = forward(1, right)
     left = product / alpha1 - alpha1 * left
-    sums[me] = jnp.broadcast_to(total(left * left), (8, 128))
-
-    def sum_copy(step):
-        return to_peer(sums.at[me], sums.at[me], sum_sem, (step,), step)
-
-    for step in range(1, npath):
-        sum_copy(step).start()
-
     state = prior[own, :] / alpha1
     rho = jnp.sqrt(alpha0 * alpha0 + beta1 * beta1)
     cosine, sine = alpha0 / rho, beta1 / rho
@@ -308,39 +310,33 @@
     search = state - theta / rho * search
 
     def keep(block, base):
-        lines = block.shape[0]
         for h in range(2):
-            pack_ref[pl.ds(base + h, lines, stride=2), :] = block[:, h * 128 : h * 128 + 128]
-
-    result_lines = pack_ref.shape[0] - 2 * CT_DEV
-    keep(state, result_lines)
-
-    for step in range(1, npath):
-        sum_copy(step).wait()
-    norm = sums[0]
-    for p in range(1, npath):
-        norm = norm + sums[p]
-    beta2 = jnp.sqrt(norm[:1, :1] + 1e-12)
+            pack_ref[pl.ds(base + h, block.shape[0], stride=2), :] = block[:, h * 128 : h * 128 + 128]
+
+    cells_end = 2 * CT_DEV
+    rows_end = cells_end + 2 * half_rows
+    keep(state, rows_end + 8)
+
+    for step in range(1, npath):
+        for far in range(2):
+            sum_copy(step, far).wait()
+    norm = total(left * left)
+    for step in range(1, npath):
+        p = sender(step)
+        whole = sums[p, 0].astype(F32) + sums[p, 1].astype(F32)
+        kept = terms[1, p, slots:, :].astype(F32)
+        kept = (kept[:8] + kept[8:]) / beta1
+        kept = jnp.concatenate([kept[:, :128], kept[:, 128:]], axis=0)
+        whole = whole / alpha1 - alpha1 * kept
+        norm = norm + total(whole * whole)
+    beta2 = jnp.sqrt(norm + 1e-12)
     left = left / beta2 * jnp.sqrt(F32(npath * half_rows * tile))
     rho = jnp.sqrt(rhobar * rhobar + beta2 * beta2)
     phi = rhobar / rho * phibar
     answer = first + phi / rho * search
     keep(answer, 0)
-    keep(left, 2 * CT_DEV)
-    pack_ref[result_lines - 8 : result_lines] = jnp.broadcast_to(beta2, (8, 128))
-
-
-def unpack(pack_ref, answer_hbm, left_hbm, sem):
-    base = 0
-    copies = []
-    for i, ref in enumerate((answer_hbm, left_hbm)):
-        part = pack_ref.at[pl.ds(base, ref.shape[0])]
-        copies.append(pltpu.make_async_copy(part, ref, sem.at[i]))
-        base += ref.shape[0]
-    for copy in copies:
-        copy.start()
-    for copy in copies:
-        copy.wait()
+    keep(left, cells_end)
+    pack_ref[rows_end : rows_end + 8] = jnp.broadcast_to(beta2, (8, 128))
 
 
 def last_right_step(tiles, tile_rows, tile_cols, tile_counts, left, beta, state):
@@ -380,7 +376,7 @@
             pltpu.VMEM((2, npath, slots + 16, tile), BF16),
             pltpu.VMEM((2, 8, tile + 128), F32),
             pltpu.VMEM((2, 8, tile + 128), F32),
-            pltpu.VMEM((npath, 8, 128), F32),
+            pltpu.VMEM((npath, 2, 16, 128), BF16),
             pltpu.VMEM((2 * slots, tile), BF16),
             pltpu.VMEM((lines, width), BF16),
             pltpu.VMEM((slots // GROUP, GROUP, tile), F32),
@@ -390,7 +386,7 @@
             pltpu.SemaphoreType.DMA((2, npath)),
             pltpu.SemaphoreType.DMA((2, 2, chunks + 1, npath)),
             pltpu.SemaphoreType.DMA((2, 2)),
-            pltpu.SemaphoreType.DMA((2, npath)),
+            pltpu.SemaphoreType.DMA((2, 2, npath)),
         ],
         compiler_params=pltpu.CompilerParams(
             collective_id=0, has_side_effects=True, vmem_limit_bytes=VMEM_LIMIT
@@ -407,26 +403,17 @@
         tile_counts,
         data.reshape(-1, 128),
     )
-    answer, left = pl.pallas_call(
-        unpack,
-        out_shape=(
-            jax.ShapeDtypeStruct((answer_lines, 128), F32),
-            jax.ShapeDtypeStruct((left_lines, 128), F32),
-        ),
-        in_specs=[vmem],
-        out_specs=(hbm, hbm),
-        scratch_shapes=[pltpu.SemaphoreType.DMA((2,))],
-    )(pack)
-    left = left.reshape(-1)
-    state = pack[answer_lines + left_lines + 8 :].reshape(CT_DEV, tile)
+    answer = pack[:answer_lines]
+    left = pack[answer_lines : answer_lines + left_lines].reshape(-1)
+    rest = pack[answer_lines + left_lines :]
     last_right_step(
         tiles,
         tile_rows,
         tile_cols,
         tile_counts,
         left / jnp.sqrt(F32(row_tiles * tile * npath)),
-        pack[answer_lines + left_lines, 0],
-        state,
+        rest[0, 0],
+        rest[8:].reshape(CT_DEV, tile),
     )
     return answer.reshape(-1), left
 

time: 34.8 us -> 33 us (0.948)
  Pallas kernels: 32.7 us -> 30.4 us
  local copies, waits for them, and re-layouts: 0.61 us -> 1.22 us
    pallas_call x1 -> x0, Pallas kernels: 1.52 us -> none  [on_device(): pl.pallas_call(unpack, out_shape=(jax.ShapeDtypeStruct((answer_lines, 128...]
    reshape x0 -> x2, local copies, waits for them, and re-layouts: none -> 1.22 us  [the longest x1 0.62 us: on_device(): return (answer.reshape(-1), left)]
    pallas_call x1, Pallas kernels: 31.2 us -> 30.4 us  [on_device(): pl.pallas_call(functools.partial(kernel, npath), out_shape=pltpu.VMEM((2...]
    unnamed x2 -> x0, local copies, waits for them, and re-layouts: 0.61 us -> none
where the time goes in v4:
time: 33 us; the launch traced here: 32.9 us
  Pallas kernels  30.4 us (92%)
  between operations  1.29 us (4%)
  local copies, waits for them, and re-layouts  1.22 us (4%)
    pallas_call x1, Pallas kernels, on_device(): pl.pallas_call(functools.partial(kernel, npath), out_shape=pltpu.VMEM((2...  30.4 us

profile of v4, /device:TPU:0, one launch (start us, length us, event | category | flops | bytes accessed | tf_op | source)
XLA Modules:
  0.0 32.9 jit_solution(16146334659981685941)
XLA Ops:
  1.3 30.4 %shard_map.68 = f32[152,128]{1,0:T(8,128)S(1)} custom-call(bf16[64,256,256]{2,1,0:T(8,128)(2,1)} %tiles_hbm.1, s32[1,64]{1,0:T(1,128)} %bitcast.8, s32[1,64]{1,0:T(1,128)} %bitcast.9, s32[1]{0:T(128)S(6)} %copy.7.counts_hbm, f32[16,128]{1,0:T(8,128)} %bitcast.7), custom_call_target="tpu_custom_call" | custom-call | flops 536870912 | bytes 8388608 | tf_op jit(solution)/shard_map/pallas_call | solution.py:364
  31.7 0.6 %slice_bitcast_fusion.1 = f32[2048]{0:T(1024)} fusion(f32[152,128]{1,0:T(8,128)S(1)} %shard_map.68), kind=kLoop, calls=%fused_computation.1 | loop fusion | bytes 16384 | tf_op jit(solution)/shard_map/reshape | solution.py:407
  32.3 0.6 %slice_bitcast_fusion = f32[8192]{0:T(1024)} fusion(f32[152,128]{1,0:T(8,128)S(1)} %shard_map.68), kind=kLoop, calls=%fused_computation | loop fusion | bytes 65536 | tf_op jit(solution)/shard_map/reshape | solution.py:418

commit v5 on v4

--- a/solution.py
+++ b/solution.py
@@ -197,7 +197,7 @@
                 term_copy(which, chunk, step).start()
             return carry
 
-        lax.fori_loop(0, chunks, one_chunk, 0)
+        lax.fori_loop(0, chunks, one_chunk, 0, unroll=2)
 
     def wait_terms(which):
         for chunk in range(chunks):
@@ -234,7 +234,7 @@
                 prods[g] = acc[:8] + acc[8:]
             return carry
 
-        lax.fori_loop(0, groups // 2, two_groups, 0)
+        lax.fori_loop(0, groups // 2, two_groups, 0, unroll=2)
         hi, lo = split(prods[...])
         both = jnp.concatenate([hi, lo], axis=1).reshape(2 * slots, tile).astype(BF16)
         acc = jnp.dot(sum_rows, both, preferred_element_type=F32)

time: 33 us -> 32.6 us (0.988)
  Pallas kernels: 30.4 us -> 29.9 us
    pallas_call x1, Pallas kernels: 30.4 us -> 29.9 us  [on_device(): pl.pallas_call(functools.partial(kernel, npath), out_shape=pltpu.VMEM((2...]
where the time goes in v5:
time: 32.6 us; the launch traced here: 32.4 us
  Pallas kernels  29.9 us (92%)
  between operations  1.29 us (4%)
  local copies, waits for them, and re-layouts  1.22 us (4%)
    pallas_call x1, Pallas kernels, on_device(): pl.pallas_call(functools.partial(kernel, npath), out_shape=pltpu.VMEM((2...  29.9 us

profile of v5, /device:TPU:0, one launch (start us, length us, event | category | flops | bytes accessed | tf_op | source)
XLA Modules:
  0.0 32.4 jit_solution(11590898888230471622)
XLA Ops:
  1.3 29.9 %shard_map.68 = f32[152,128]{1,0:T(8,128)S(1)} custom-call(bf16[64,256,256]{2,1,0:T(8,128)(2,1)} %tiles_hbm.1, s32[1,64]{1,0:T(1,128)} %bitcast.8, s32[1,64]{1,0:T(1,128)} %bitcast.9, s32[1]{0:T(128)S(6)} %copy.7.counts_hbm, f32[16,128]{1,0:T(8,128)} %bitcast.7), custom_call_target="tpu_custom_call" | custom-call | flops 536870912 | bytes 8388608 | tf_op jit(solution)/shard_map/pallas_call | solution.py:364
  31.2 0.6 %slice_bitcast_fusion.1 = f32[2048]{0:T(1024)} fusion(f32[152,128]{1,0:T(8,128)S(1)} %shard_map.68), kind=kLoop, calls=%fused_computation.1 | loop fusion | bytes 16384 | tf_op jit(solution)/shard_map/reshape | solution.py:407
  31.8 0.6 %slice_bitcast_fusion = f32[8192]{0:T(1024)} fusion(f32[152,128]{1,0:T(8,128)S(1)} %shard_map.68), kind=kLoop, calls=%fused_computation | loop fusion | bytes 65536 | tf_op jit(solution)/shard_map/reshape | solution.py:418
